TPU v7x, 128 devices: a whole 4x4x4 slice. The times are simulated.
128 devices in a mesh: sec: 32 (over z, y, x_hi), tpl: 4 (over x_lo, core).
Axes of the slice: x: 4 (x_hi: 2, x_lo: 2; x = x_hi * 2 + x_lo), y: 4, z: 4, core: 2. Of those that a mesh axis runs over, the one named last changes fastest.
Arguments:
- raw: float32 [24576, 899], P('sec'), may hold values from -6 to 6
- stencil: float32 [3, 5], replicated, may hold values from -1.5 to 1.5
- mad: float32 [24576], P('sec'), may hold values from 0.5 to 4
- templates: bfloat16 [2048, 512], P(('sec', 'tpl')), may hold values from -0.25 to 0.25
- shifts: int32 [2048, 32], P(None, 'sec'), may hold values from 0 to 256
- listed: int32 [32, 128], P('sec', 'tpl'), may hold values from 0 to 2047, as said below
- counts: int32 [32, 4], P('sec', 'tpl'), may hold values from 16 to 32, as said below
Outputs:
- stack: float32 [2048, 128], P(('sec', 'tpl'))
Inputs may be any that keep to these rules, and one draw needn't show every extreme that they name: `listed`: each device's 32 entries (live or not) name templates of 32 different owners, template k being owned by device k // 16 along sec+tpl; so no two entries of one device's list lie in the same owner's rows. `counts`: one device has 32 live slots.
All inputs are finite; a program needn't handle non-finite values.
Results may differ from a plain program's by a relative error of at most 0.0034.
Values may be sent and summed in bfloat16 or wider, within the bound.
A program may use at most 64 MiB of HBM per device.

v0:
```python
import jax
import jax.numpy as jnp
from jax import lax
from jax.sharding import PartitionSpec as P

LAGS = 128
PER_OWNER = 1


def with_halo(cells, sides, width):
    for axis, dim in sides:
        count = lax.axis_size(axis)
        ends = count - 1
        head = lax.slice_in_dim(cells, 0, width, axis=dim)
        tail = lax.slice_in_dim(cells, cells.shape[dim] - width, cells.shape[dim], axis=dim)
        cells = jnp.concatenate(
            [
                lax.ppermute(tail, axis, [(i, (i + 1) % count) for i in range(ends)]),
                cells,
                lax.ppermute(head, axis, [((i + 1) % count, i) for i in range(ends)]),
            ],
            axis=dim,
        )
    return cells


def robust(value):
    return value * lax.rsqrt(1.0 + value * value)


def banded(block, tpl_len):
    number = block.shape[0]
    period = tpl_len + 128
    widened = jnp.concatenate([block, jnp.zeros((number, 128), block.dtype)], axis=1)
    repeated = jnp.tile(widened, (1, 128))[:, : 128 * (period - 1)]
    return repeated.reshape(number, 128, period - 1)


def shifted(series, offset):
    return lax.dynamic_slice_in_dim(series, offset, LAGS)


def shards(raw, stencil, mad, templates, shifts, listed, counts):
    channels = raw.shape[0]
    window = raw.shape[1] - 4
    tpl_len = templates.shape[1]
    own_rows = templates.shape[0]
    catalog = shifts.shape[0]
    slots = listed.shape[1]
    devices = lax.axis_size(("sec", "tpl"))
    lag_ext = window - tpl_len + 1
    lag_tiles = lag_ext // 128
    band_len = 128 + tpl_len - 1
    padded = with_halo(raw, (("sec", 0),), 1)
    filtered = jnp.zeros((channels, window), jnp.float32)
    for across in range(3):
        for along in range(5):
            filtered = (
                filtered
                + stencil[across, along]
                * padded[across : across + channels, along : along + window]
            )
    whitened = (filtered / mad[:, None]).astype(jnp.bfloat16)
    names = listed[0]
    alive = jnp.arange(slots, dtype=jnp.int32) < counts[0, 0]
    match = names[:, None] == jnp.arange(catalog, dtype=jnp.int32)[None, :]
    offsets = jnp.sum(jnp.where(match, shifts[:, 0][None, :], 0), axis=1)
    owners = names // own_rows
    earlier = jnp.arange(slots)[None, :] < jnp.arange(slots)[:, None]
    same_owner = (owners[:, None] == owners[None, :]) & alive[None, :] & earlier
    rank = jnp.sum(same_owner.astype(jnp.int32), axis=1)
    target = owners * PER_OWNER + rank
    places = (jnp.arange(devices * PER_OWNER, dtype=jnp.int32)[:, None] == target[None, :]) & alive[
        None, :
    ]
    wanted = jnp.sum(jnp.where(places, names[None, :] + 1, 0), axis=1) - 1
    piece = lax.all_gather(templates, ("sec", "tpl"), axis=0, tiled=True)
    index = jnp.arange(piece.shape[0], dtype=jnp.int32)
    onehot = (names[:, None] == index[None, :]).astype(jnp.bfloat16)
    chosen = jnp.dot(onehot, piece, preferred_element_type=jnp.float32).astype(jnp.bfloat16)
    segments = jnp.stack(
        [whitened[:, number * 128 : number * 128 + band_len] for number in range(lag_tiles)]
    )

    def one_block(unused, block):
        matrix = banded(block, tpl_len)
        corr = jnp.einsum("mci,kti->mckt", segments, matrix, preferred_element_type=jnp.float32)
        summed = jnp.sum(robust(corr), axis=1)
        return (unused, jnp.transpose(summed, (1, 0, 2)).reshape(block.shape[0], lag_ext))

    _, lagged = lax.scan(
        one_block, jnp.zeros((), jnp.float32), chosen.reshape(slots // 4, 4, tpl_len)
    )
    lagged = lagged.reshape(slots, lag_ext)
    partial_value = jax.vmap(shifted)(lagged, offsets)
    partial_value = jnp.where(alive[:, None], partial_value, jnp.zeros_like(partial_value))
    send_rows = jnp.dot(
        places.astype(jnp.float32), partial_value, precision=lax.Precision.HIGHEST
    ).reshape(devices, PER_OWNER, LAGS)
    got_rows, got_names = (
        lax.all_to_all(send_rows, ("sec", "tpl"), split_axis=0, concat_axis=0, tiled=True),
        lax.all_to_all(
            wanted.reshape(devices, PER_OWNER),
            ("sec", "tpl"),
            split_axis=0,
            concat_axis=0,
            tiled=True,
        ),
    )
    flat_names = got_names.reshape(-1)
    into = (
        (flat_names[None, :] % own_rows == jnp.arange(own_rows, dtype=jnp.int32)[:, None])
        & (flat_names[None, :] >= 0)
    ).astype(jnp.float32)
    total = jnp.dot(into, got_rows.reshape(-1, LAGS), precision=lax.Precision.HIGHEST)
    tally = jnp.sum(into, axis=1)
    return total / jnp.sqrt(jnp.maximum(tally, 1.0) * channels)[:, None]


def solution(mesh):
    in_specs = (
        P("sec", None),
        P(),
        P("sec"),
        P(("sec", "tpl"), None),
        P(None, "sec"),
        P("sec", "tpl"),
        P("sec", "tpl"),
    )
    out_specs = P(("sec", "tpl"), None)
    return jax.shard_map(shards, mesh=mesh, in_specs=in_specs, out_specs=out_specs, check_vma=False)
```

profile of v0, /device:TPU:1, one launch (start us, length us, event | category | flops | bytes accessed | tf_op | source)
XLA Modules:
  0.0 227.5 jit_solution(4315780559564731957)
XLA Ops:
  6.6 2.3 %copy.49 = f32[768,899]{1,0:T(8,128)S(1)} copy(f32[768,899]{0,1:T(8,128)} %param.9) | data formatting | bytes 5523456 | tf_op args[0]
  8.9 5.5 %collective-permute-start = (f32[1,899]{1,0:T(1,128)S(1)}, f32[1,899]{1,0:T(1,128)S(1)}, u32[]{:S(2)}, u32[]{:S(2)}) collective-permute-start(f32[1,899]{1,0:T(1,128)S(1)} %get-tuple-element.54), channel_id=1, source_target_pairs={{0,4},{4,8},{8,12},{12,16},{16,20},{20,24},{24,28},{28,32},{32,36}... | collective-permute-start | bytes 10796 | tf_op jit(solution)/shard_map/ppermute | solution.py:18
  14.4 1.3 collective-permute-start.1
  17.5 12.1 %all-to-all-start = ((s32[128,1,1]{2,1,0:T(1,128)}), s32[128,1,1]{2,1,0:T(1,128)S(1)}, u32[]{:S(2)}, u32[]{:S(2)}) async-start(s32[128,1,1]{2,1,0:T(1,128)} %copy.48), calls=%async_computation | async-start | bytes 131072 | tf_op jit(solution)/shard_map/all_to_all | solution.py:102
  30.5 8.6 %all-to-all-done = s32[128,1,1]{2,1,0:T(1,128)S(1)} async-done(((s32[128,1,1]{2,1,0:T(1,128)}), s32[128,1,1]{2,1,0:T(1,128)S(1)}, u32[]{:S(2)}, u32[]{:S(2)}) %all-to-all-start) | async-done | bytes 544 | tf_op jit(solution)/shard_map/all_to_all | solution.py:102
  39.2 2.3 %reduce = s32[128]{0:T(128)S(1)} reduce(s32[128,1,1]{2,1,0:T(1,128)S(1)} %all-to-all-done, s32[]{:T(128)} %copy.79), dimensions={1,2}, to_apply=%all_to_all.7.reduce_sub_computation | reduce | bytes 1028 | tf_op jit(solution)/shard_map/all_to_all | solution.py:102
  41.7 21.5 %fusion.41 = bf16[768,895]{1,0:T(8,128)(2,1)S(1)} fusion(f32[1,899]{1,0:T(1,128)S(1)} %collective-permute-done.1, f32[768,899]{1,0:T(8,128)S(1)} %copy.49, f32[1,899]{1,0:T(1,128)S(1)} %collective-permute-done, f32[768]{0:T(1024)S(1)} %copy-done.2, f32[]{:T(128)} %bitcast.26, f32[]{:T(128)} %bitcast.25, f32[]{:T(128)} %bitcast.24, f32[]{:T(128)} %bitcast.23, ...), kind=kLoop, calls=%fused_computation.65 | loop fusion | flops 28181760 | bytes 18295356 | tf_op jit(solution)/shard_map/convert_element_type | solution.py:63
  63.5 2.1 pad_maximum_fusion
  65.6 19.8 %all-gather.2.cloned.1.call-done = bf16[2048,512]{1,0:T(8,128)(2,1)} async-done(((bf16[16,512]{1,0:T(8,128)(2,1)}), bf16[2048,512]{1,0:T(8,128)(2,1)}) %all-gather.2.cloned.1.call-update) | async-done | bytes 2097168 | tf_op jit(solution)/shard_map/all_gather | solution.py:77
  85.4 2.1 convolution_convert_fusion
  87.5 51.3 %while.13 = (s32[]{:T(128)}, f32[8,4,384]{2,1,0:T(4,128)S(1)}, bf16[8,4,512]{2,1,0:T(4,128)(2,1)S(1)}, bf16[3,768,639]{2,1,0:T(8,128)(2,1)}) while((s32[]{:T(128)}, f32[8,4,384]{2,1,0:T(4,128)S(1)}, bf16[8,4,512]{2,1,0:T(4,128)(2,1)S(1)}, bf16[3,768,639]{2,1,0:T(8,128)(2,1)}) %tuple.57), condition=%wide.region_4.5_spmd.clone, body=%wide.region_2.4_spmd.sunk.clone | while | flops 1512307200 | bytes 8235583 | solution.py:91
  88.4 1.5 reshape.158
  89.9 4.0 %fusion.74 = f32[3,4,128]{2,0,1:T(4,128)S(1)} fusion(bf16[3,768,639]{2,1,0:T(8,128)(2,1)} %get-tuple-element.165, bf16[4,128,639,1]{2,1,0,3:T(8,128)(2,1)S(1)} %reshape.158), kind=kOutput, calls=%fused_computation.4.clone.1.clone | convolution fusion | flops 1512307200 | bytes 3604992 | tf_op jit(solution)/shard_map/while/body/eval_jaxpr/mci,kti->mckt/dot_general | solution.py:87
  94.8 1.5 reshape.158
  96.3 4.0 %fusion.74 = f32[3,4,128]{2,0,1:T(4,128)S(1)} fusion(bf16[3,768,639]{2,1,0:T(8,128)(2,1)} %get-tuple-element.165, bf16[4,128,639,1]{2,1,0,3:T(8,128)(2,1)S(1)} %reshape.158), kind=kOutput, calls=%fused_computation.4.clone.1.clone | convolution fusion | flops 1512307200 | bytes 3604992 | tf_op jit(solution)/shard_map/while/body/eval_jaxpr/mci,kti->mckt/dot_general | solution.py:87
  101.2 1.5 reshape.158
  102.7 4.0 %fusion.74 = f32[3,4,128]{2,0,1:T(4,128)S(1)} fusion(bf16[3,768,639]{2,1,0:T(8,128)(2,1)} %get-tuple-element.165, bf16[4,128,639,1]{2,1,0,3:T(8,128)(2,1)S(1)} %reshape.158), kind=kOutput, calls=%fused_computation.4.clone.1.clone | convolution fusion | flops 1512307200 | bytes 3604992 | tf_op jit(solution)/shard_map/while/body/eval_jaxpr/mci,kti->mckt/dot_general | solution.py:87
  107.6 1.5 reshape.158
  109.1 4.0 %fusion.74 = f32[3,4,128]{2,0,1:T(4,128)S(1)} fusion(bf16[3,768,639]{2,1,0:T(8,128)(2,1)} %get-tuple-element.165, bf16[4,128,639,1]{2,1,0,3:T(8,128)(2,1)S(1)} %reshape.158), kind=kOutput, calls=%fused_computation.4.clone.1.clone | convolution fusion | flops 1512307200 | bytes 3604992 | tf_op jit(solution)/shard_map/while/body/eval_jaxpr/mci,kti->mckt/dot_general | solution.py:87
  114.0 1.5 reshape.158
  115.5 4.0 %fusion.74 = f32[3,4,128]{2,0,1:T(4,128)S(1)} fusion(bf16[3,768,639]{2,1,0:T(8,128)(2,1)} %get-tuple-element.165, bf16[4,128,639,1]{2,1,0,3:T(8,128)(2,1)S(1)} %reshape.158), kind=kOutput, calls=%fused_computation.4.clone.1.clone | convolution fusion | flops 1512307200 | bytes 3604992 | tf_op jit(solution)/shard_map/while/body/eval_jaxpr/mci,kti->mckt/dot_general | solution.py:87
  120.4 1.5 reshape.158
  121.9 4.0 %fusion.74 = f32[3,4,128]{2,0,1:T(4,128)S(1)} fusion(bf16[3,768,639]{2,1,0:T(8,128)(2,1)} %get-tuple-element.165, bf16[4,128,639,1]{2,1,0,3:T(8,128)(2,1)S(1)} %reshape.158), kind=kOutput, calls=%fused_computation.4.clone.1.clone | convolution fusion | flops 1512307200 | bytes 3604992 | tf_op jit(solution)/shard_map/while/body/eval_jaxpr/mci,kti->mckt/dot_general | solution.py:87
  126.8 1.5 reshape.158
  128.3 4.0 %fusion.74 = f32[3,4,128]{2,0,1:T(4,128)S(1)} fusion(bf16[3,768,639]{2,1,0:T(8,128)(2,1)} %get-tuple-element.165, bf16[4,128,639,1]{2,1,0,3:T(8,128)(2,1)S(1)} %reshape.158), kind=kOutput, calls=%fused_computation.4.clone.1.clone | convolution fusion | flops 1512307200 | bytes 3604992 | tf_op jit(solution)/shard_map/while/body/eval_jaxpr/mci,kti->mckt/dot_general | solution.py:87
  133.2 1.5 reshape.158
  134.7 4.0 %fusion.74 = f32[3,4,128]{2,0,1:T(4,128)S(1)} fusion(bf16[3,768,639]{2,1,0:T(8,128)(2,1)} %get-tuple-element.165, bf16[4,128,639,1]{2,1,0,3:T(8,128)(2,1)S(1)} %reshape.158), kind=kOutput, calls=%fused_computation.4.clone.1.clone | convolution fusion | flops 1512307200 | bytes 3604992 | tf_op jit(solution)/shard_map/while/body/eval_jaxpr/mci,kti->mckt/dot_general | solution.py:87
  138.8 65.2 %while.14 = (s32[]{:T(128)}, f32[32,384]{1,0:T(8,128)S(1)}, s32[32,2]{0,1:T(2,128)S(1)}, f32[32,128]{1,0:T(8,128)S(1)}) while((s32[]{:T(128)}, f32[32,384]{1,0:T(8,128)S(1)}, s32[32,2]{0,1:T(2,128)S(1)}, f32[32,128]{1,0:T(8,128)S(1)}) %tuple.60), condition=%wide.while_cond.clone, body=%wide.while_body.sunk.clone | while | flops 2 | bytes 2145 | solution.py:40
  139.5 1.4 dynamic-slice.9
  141.5 1.4 dynamic-slice.9
  143.6 1.4 dynamic-slice.9
  145.6 1.4 dynamic-slice.9
  147.7 1.4 dynamic-slice.9
  149.7 1.4 dynamic-slice.9
  151.7 1.4 dynamic-slice.9
  153.8 1.4 dynamic-slice.9
  155.8 1.4 dynamic-slice.9
  157.8 1.4 dynamic-slice.9
  159.9 1.4 dynamic-slice.9
  161.9 1.4 dynamic-slice.9
  164.0 1.4 dynamic-slice.9
  166.0 1.4 dynamic-slice.9
  168.0 1.4 dynamic-slice.9
  170.1 1.4 dynamic-slice.9
  172.1 1.4 dynamic-slice.9
  174.1 1.4 dynamic-slice.9
  176.2 1.4 dynamic-slice.9
  178.2 1.4 dynamic-slice.9
  180.3 1.4 dynamic-slice.9
  182.3 1.4 dynamic-slice.9
  184.3 1.4 dynamic-slice.9
  186.4 1.4 dynamic-slice.9
  188.4 1.4 dynamic-slice.9
  190.4 1.4 dynamic-slice.9
  192.5 1.4 dynamic-slice.9
  194.5 1.4 dynamic-slice.9
  196.6 1.4 dynamic-slice.9
  198.6 1.4 dynamic-slice.9
  200.6 1.4 dynamic-slice.9
  202.7 1.4 dynamic-slice.9
  204.1 0.9 fusion.43
  205.0 5.3 %all-to-all-start.1 = ((f32[128,1,128]{2,1,0:T(1,128)}), f32[128,1,128]{2,1,0:T(1,128)S(1)}, u32[]{:S(2)}, u32[]{:S(2)}) async-start(f32[128,1,128]{2,1,0:T(1,128)} %bitcast.33), calls=%async_computation.1 | async-start | bytes 131072 | tf_op jit(solution)/shard_map/all_to_all | solution.py:101
  210.3 9.6 %all-to-all-done.1 = f32[128,1,128]{2,1,0:T(1,128)S(1)} async-done(((f32[128,1,128]{2,1,0:T(1,128)}), f32[128,1,128]{2,1,0:T(1,128)S(1)}, u32[]{:S(2)}, u32[]{:S(2)}) %all-to-all-start.1) | async-done | bytes 65568 | tf_op jit(solution)/shard_map/all_to_all | solution.py:101
  219.9 0.8 convolution_divide_fusion
  (187 shorter events, 31.0 us)
Async XLA Ops:
  6.5 9.2 %copy-start.3 = (s32[1,32]{1,0:T(1,128)S(1)}, s32[1,32]{1,0:T(1,128)}, u32[]{:S(2)}) copy-start(s32[1,32]{1,0:T(1,128)} %param.14) | copy-start | bytes 388
  6.5 23.0 %copy-start = (f32[3,5]{1,0:T(4,128)S(1)}, f32[3,5]{1,0:T(4,128)}, u32[]{:S(2)}) copy-start(f32[3,5]{1,0:T(4,128)} %param.10) | copy-start | bytes 184
  6.5 23.7 %copy-start.1 = (s32[2048,1]{0,1:T(1,128)S(1)}, s32[2048,1]{0,1:T(1,128)}, u32[]{:S(2)}) copy-start(s32[2048,1]{0,1:T(1,128)} %param.13) | copy-start | bytes 24580
  6.5 35.1 %copy-start.2 = (f32[768]{0:T(1024)S(1)}, f32[768]{0:T(1024)}, u32[]{:S(2)}) copy-start(f32[768]{0:T(1024)} %param.11) | copy-start | bytes 9220
  6.5 78.9 %all-gather.2.cloned.1.call-start = ((), (), s32[]{:S(2)}) async-start(), calls=%async_computation.2 | async-start | bytes 2113536 | tf_op jit(solution)/shard_map/all_gather | solution.py:77
  8.9 32.7 %collective-permute-start = (f32[1,899]{1,0:T(1,128)S(1)}, f32[1,899]{1,0:T(1,128)S(1)}, u32[]{:S(2)}, u32[]{:S(2)}) collective-permute-start(f32[1,899]{1,0:T(1,128)S(1)} %get-tuple-element.54), channel_id=1, source_target_pairs={{0,4},{4,8},{8,12},{12,16},{16,20},{20,24},{24,28},{28,32},{32,36}... | collective-permute-start | bytes 10796 | tf_op jit(solution)/shard_map/ppermute | solution.py:18
  14.4 27.3 %collective-permute-start.1 = (f32[1,899]{1,0:T(1,128)S(1)}, f32[1,899]{1,0:T(1,128)S(1)}, u32[]{:S(2)}, u32[]{:S(2)}) collective-permute-start(f32[1,899]{1,0:T(1,128)S(1)} %get-tuple-element.55), channel_id=1, source_target_pairs={{4,0},{8,4},{12,8},{16,12},{20,16},{24,20},{28,24},{32,28},{36,32}... | collective-permute-start | bytes 10796 | tf_op jit(solution)/shard_map/ppermute | solution.py:20
  17.5 21.7 %all-to-all-start = ((s32[128,1,1]{2,1,0:T(1,128)}), s32[128,1,1]{2,1,0:T(1,128)S(1)}, u32[]{:S(2)}, u32[]{:S(2)}) async-start(s32[128,1,1]{2,1,0:T(1,128)} %copy.48), calls=%async_computation | async-start | bytes 131072 | tf_op jit(solution)/shard_map/all_to_all | solution.py:102
  205.0 14.9 %all-to-all-start.1 = ((f32[128,1,128]{2,1,0:T(1,128)}), f32[128,1,128]{2,1,0:T(1,128)S(1)}, u32[]{:S(2)}, u32[]{:S(2)}) async-start(f32[128,1,128]{2,1,0:T(1,128)} %bitcast.33), calls=%async_computation.1 | async-start | bytes 131072 | tf_op jit(solution)/shard_map/all_to_all | solution.py:101
Sparse Core Ops, SparseCore 0:
  15.9 69.5 all-gather.1
where the time goes:
time: 229 us; the launch traced here: 228 us
  local copies, waits for them, and re-layouts  87.8 us (38%)
  waiting for transfers between devices  38.1 us (17%)
  matrix products  36 us (16%)
  other arithmetic  26.6 us (12%)
  starting transfers between devices  24.2 us (11%)
  between operations  14.2 us (6%)
    gather x128, local copies, waits for them, and re-layouts  65.1 us
    dot_general x8, matrix products, one_block(): jnp.einsum('mci,kti->mckt', segments, matrix, preferred_element_type=jnp....  32.2 us
    convert_element_type x1, other arithmetic, shards(): whitened = (filtered / mad[:, None]).astype(jnp.bfloat16)  21.5 us
    all_gather x1, waiting for transfers between devices, shards(): piece = lax.all_gather(templates, ('sec', 'tpl'), axis=0, tiled=True)  19.8 us
    all_to_all x1, starting transfers between devices, shards(): lax.all_to_all(wanted.reshape(devices, PER_OWNER), ('sec', 'tpl'), split_...  12.1 us
    reshape x8, local copies, waits for them, and re-layouts, banded(): return repeated.reshape(number, 128, period - 1)  11.9 us
    all_to_all x1, waiting for transfers between devices, shards(): lax.all_to_all(send_rows, ('sec', 'tpl'), split_axis=0, concat_axis=0, ti...  9.59 us
    all_to_all x1, waiting for transfers between devices, shards(): lax.all_to_all(wanted.reshape(devices, PER_OWNER), ('sec', 'tpl'), split_...  8.63 us
  transfers between devices with their start and end apart: 5, of which 3 were waited for; matrix products, arithmetic and copies ran while one was open for 12% of the time, Pallas kernels for 0%

commit v1 on v0

v1 whole, which is shorter than its diff:
```python
import functools

import jax
import jax.numpy as jnp
from jax import lax
from jax.experimental import pallas as pl
from jax.experimental.pallas import tpu as pltpu
from jax.sharding import PartitionSpec as P

MESH = pl.DeviceIdType.MESH
DEVICES = 128
CHAN = 768
LAGS = 128
TLEN = 512
SLOTS = 32
OWN = 16
WINDOW = 768
WIDTH = 896
PAIRS = SLOTS // 2 + 1
NT = (((1,), (1,)), ((), ()))
TN = (((0,), (0,)), ((), ()))


def hops(step):
    return sum((0, 1, 2, 1)[d] for d in step[:3]) + 0.1 * step[3]


STEPS = sorted(
    [
        (dz, dy, dx, dc)
        for dz in range(4)
        for dy in range(4)
        for dx in range(4)
        for dc in range(2)
        if (dz, dy, dx, dc) != (0, 0, 0, 0)
    ],
    key=hops,
    reverse=True,
)


def peers():
    sec = lax.axis_index("sec")
    tpl = lax.axis_index("tpl")
    z = sec // 8
    y = sec // 2 % 4
    x = sec % 2 * 2 + tpl // 2
    core = tpl % 2
    zs = [(z + d) % 4 * 8 for d in range(4)]
    ys = [(y + d) % 4 * 2 for d in range(4)]
    xs = [(x + d) % 4 for d in range(4)]
    his = [v // 2 for v in xs]
    los = [v % 2 * 2 for v in xs]
    cores = [(core + d) % 2 for d in range(2)]
    out = []
    for dz, dy, dx, dc in STEPS:
        s = zs[dz] + ys[dy] + his[dx]
        t = los[dx] + cores[dc]
        out.append((s, t))
    return sec, tpl, out


def robust(value):
    return value * lax.rsqrt(1.0 + value * value)


def build(rows, shift):
    flat = jnp.concatenate(
        [jnp.broadcast_to(rows[k : k + 1], (8, 128)) for k in range(4)]
        + [jnp.zeros((8, WINDOW - TLEN), jnp.float32)],
        axis=1,
    )
    base = pltpu.roll(flat, shift, 1)
    base = pltpu.roll(base, 0, 1, stride=1, stride_axis=0)
    both = jnp.concatenate([base, pltpu.roll(base, 8, 1)], axis=0).astype(jnp.bfloat16)
    return jnp.concatenate([pltpu.roll(both, 16 * g, 1) if g else both for g in range(8)], axis=0)


def kernel(
    raw_ref,
    stencil_ref,
    mad_ref,
    templates_ref,
    shifts_ref,
    listed_ref,
    counts_ref,
    total_ref,
    tally_ref,
    raw_v,
    cu,
    white,
    inv_mad,
    name_out,
    name_in,
    row_out,
    row_in,
    part_out,
    part_in,
    info_v,
    info_s,
    acc,
    even_v,
    odd_v,
    *rest,
):
    bands = rest[:16]
    raw_sem, info_sem, halo_send, halo_recv, name_sems, row_sems, part_sems = rest[16:]
    sec, tpl, others = peers()
    me = sec * 4 + tpl

    load = pltpu.make_async_copy(raw_ref, raw_v, raw_sem)
    load.start()
    barrier = pltpu.get_barrier_semaphore()
    for s, t in others:
        pl.semaphore_signal(barrier, inc=1, device_id=(s, t), device_id_type=MESH)

    def send_all(src, dst, sems):
        for s, t in others:
            pltpu.make_async_remote_copy(
                src_ref=src.at[s * 4 + t],
                dst_ref=dst.at[me],
                send_sem=sems.at[0],
                recv_sem=sems.at[1],
                device_id=(s, t),
                device_id_type=MESH,
            ).start()
        pltpu.make_async_copy(src.at[me], dst.at[me], sems.at[1]).start()

    def got_all(src, dst, sems):
        pltpu.make_async_copy(src, dst, sems.at[1]).wait()

    def sent_all(src, dst, sems):
        part = pl.ds(0, DEVICES - 1)
        pltpu.make_async_copy(src.at[part], dst.at[part], sems.at[0]).wait()

    lane = lax.broadcasted_iota(jnp.int32, (SLOTS, 128), 1)
    slot = lax.broadcasted_iota(jnp.int32, (SLOTS, 128), 0)
    name = jnp.zeros((SLOTS, 128), jnp.int32)
    rest_shift = jnp.zeros((SLOTS, 128), jnp.int32)
    place = jnp.zeros((SLOTS, 128), jnp.int32)
    early_slots = jnp.int32(0)
    for q in range(SLOTS):
        k = listed_ref[0, q]
        moved = shifts_ref[k]
        late = (moved >= 128).astype(jnp.int32)
        spot = early_slots + late * (2 * PAIRS - 1 - q)
        early_slots = early_slots + 1 - late
        name = jnp.where(slot == q, k, name)
        rest_shift = jnp.where(slot == q, moved - 128 * late, rest_shift)
        place = jnp.where(slot == q, spot, place)
    owner = name // OWN
    within = name - owner * OWN
    live = slot < counts_ref[0, 0]
    own_hot = (owner == lane).astype(jnp.bfloat16)
    asked = jnp.where(live, within + 1, 0).astype(jnp.bfloat16)
    name_out[:, 0, :] = lax.dot_general(own_hot, asked, TN, preferred_element_type=jnp.float32)
    hot = place == lane
    info_v[0:1, :] = jnp.sum(jnp.where(hot, rest_shift, 0), axis=0, keepdims=True)
    info_v[1:2, :] = jnp.sum(jnp.where(hot, owner, 0), axis=0, keepdims=True)
    info_v[2:8, :] = jnp.zeros((6, 128), jnp.int32)
    info = pltpu.make_async_copy(info_v, info_s, info_sem)
    info.start()
    even_hot = (place == 2 * lane).astype(jnp.bfloat16)
    odd_hot = (place == 2 * lane + 1).astype(jnp.bfloat16)
    even_v[...] = lax.dot_general(even_hot, own_hot, TN, preferred_element_type=jnp.float32)
    odd_v[...] = lax.dot_general(odd_hot, own_hot, TN, preferred_element_type=jnp.float32)
    inv_mad[...] = jnp.broadcast_to(1.0 / mad_ref[...], (128, CHAN)).T
    acc[...] = jnp.zeros_like(acc)

    load.wait()
    for k in range(7):
        cu[8 : 8 + CHAN, 128 * k : 128 * k + 128] = raw_v[128 * k : 128 * k + 128, :].T
    tail = jnp.concatenate([raw_v[896:899, :], jnp.zeros((125, CHAN), jnp.float32)], axis=0)
    cu[8 : 8 + CHAN, 896:1024] = tail.T

    pl.semaphore_wait(barrier, DEVICES - 1)
    send_all(name_out, name_in, name_sems)
    up = pltpu.make_async_remote_copy(
        src_ref=cu.at[pl.ds(CHAN, 8)],
        dst_ref=cu.at[pl.ds(0, 8)],
        send_sem=halo_send.at[0],
        recv_sem=halo_recv.at[0],
        device_id=((sec + 1) % 32, tpl),
        device_id_type=MESH,
    )
    down = pltpu.make_async_remote_copy(
        src_ref=cu.at[pl.ds(8, 8)],
        dst_ref=cu.at[pl.ds(CHAN + 8, 8)],
        send_sem=halo_send.at[1],
        recv_sem=halo_recv.at[1],
        device_id=((sec + 31) % 32, tpl),
        device_id_type=MESH,
    )
    up.start()
    down.start()

    got_all(name_out, name_in, name_sems)
    wanted = name_in[:, 0, :]
    lanes = lax.broadcasted_iota(jnp.int32, (DEVICES, 128), 1)
    into = jnp.where(wanted.astype(jnp.int32) == lanes + 1, 1.0, 0.0)
    chosen = jnp.dot(
        into[:, :OWN].astype(jnp.bfloat16), templates_ref[...], preferred_element_type=jnp.float32
    )
    for k in range(4):
        row_out[:, k, :] = chosen[:, 128 * k : 128 * k + 128]
    send_all(row_out, row_in, row_sems)
    ones = jnp.ones((DEVICES, 128), jnp.bfloat16)
    tally = lax.dot_general(into.astype(jnp.bfloat16), ones, TN, preferred_element_type=jnp.float32)
    tally_ref[...] = tally[:OWN]

    up.wait()
    down.wait()

    def whiten(i, carry):
        base = pl.multiple_of(i * 16, 16)
        block = cu[pl.ds(base, 32), :]
        rows = lax.broadcasted_iota(jnp.int32, (16, 1024), 0) + base
        above = jnp.where((rows == 0) & (sec == 0), 0.0, block[7:23])
        below = jnp.where((rows == CHAN - 1) & (sec == 31), 0.0, block[9:25])
        middle = block[8:24]
        total = None
        for b in range(5):
            term = (
                stencil_ref[0, b] * above + stencil_ref[1, b] * middle + stencil_ref[2, b] * below
            )
            if b:
                term = pltpu.roll(term, 1024 - b, 1)
            term = term[:, :WIDTH]
            total = term if total is None else total + term
        scale = inv_mad[pl.ds(base, 16), :]
        scale = jnp.concatenate([scale] * (WIDTH // 128), axis=1)
        done = (total * scale).astype(jnp.bfloat16)
        white[0, pl.ds(base, 16), :] = done[:, :WINDOW]
        white[1, pl.ds(base, 16), :] = done[:, 128:]
        return carry

    lax.fori_loop(0, CHAN // 16, whiten, 0)

    info.wait()
    got_all(row_out, row_in, row_sems)

    def prepare(j, band):
        for h in range(2):
            rows = row_in[info_s[1, 2 * j + h]]
            band[128 * h : 128 * h + 128, :] = build(rows, info_s[0, 2 * j + h])

    def correlate(j, band):
        half = (2 * j >= early_slots).astype(jnp.int32)
        corr = lax.dot_general(white[half], band[...], NT, preferred_element_type=jnp.float32)
        acc[j] = robust(corr).reshape(CHAN // 8, 8, 256).sum(axis=0)

    for u in range(8):
        prepare(u, bands[u])
    for u in range(PAIRS):
        if u + 8 < PAIRS:
            prepare(u + 8, bands[(u + 8) % 16])
        correlate(u, bands[u % 16])

    sums = jnp.sum(acc[...], axis=1)
    part_out[:, 0, :] = lax.dot_general(
        even_v[:24], sums[:, :128], TN, precision=lax.Precision.HIGHEST,
        preferred_element_type=jnp.float32,
    ) + lax.dot_general(
        odd_v[:24], sums[:, 128:], TN, precision=lax.Precision.HIGHEST,
        preferred_element_type=jnp.float32,
    )
    send_all(part_out, part_in, part_sems)
    sent_all(name_out, name_in, name_sems)
    sent_all(row_out, row_in, row_sems)
    got_all(part_out, part_in, part_sems)
    total = lax.dot_general(
        into, part_in[:, 0, :], TN, precision=lax.Precision.HIGHEST,
        preferred_element_type=jnp.float32,
    )
    total_ref[...] = total[:OWN]
    sent_all(part_out, part_in, part_sems)


def shards(raw, stencil, mad, templates, shifts, listed, counts):
    vmem = pl.BlockSpec(memory_space=pltpu.VMEM)
    smem = pl.BlockSpec(memory_space=pltpu.SMEM)
    f32 = jnp.float32
    dma = pltpu.SemaphoreType.DMA
    out = jax.ShapeDtypeStruct((OWN, LAGS), f32)
    total, tally = pl.pallas_call(
        kernel,
        out_shape=(out, out),
        in_specs=[pl.BlockSpec(memory_space=pl.ANY), smem, vmem, vmem, smem, smem, smem],
        out_specs=(vmem, vmem),
        scratch_shapes=[
            pltpu.VMEM((899, CHAN), f32),
            pltpu.VMEM((CHAN + 16, 1024), f32),
            pltpu.VMEM((2, CHAN, WINDOW), jnp.bfloat16),
            pltpu.VMEM((CHAN, 128), f32),
            pltpu.VMEM((DEVICES, 1, 128), f32),
            pltpu.VMEM((DEVICES, 1, 128), f32),
            pltpu.VMEM((DEVICES, 4, 128), f32),
            pltpu.VMEM((DEVICES, 4, 128), f32),
            pltpu.VMEM((DEVICES, 1, 128), f32),
            pltpu.VMEM((DEVICES, 1, 128), f32),
            pltpu.VMEM((8, 128), jnp.int32),
            pltpu.SMEM((8, 128), jnp.int32),
            pltpu.VMEM((24, 8, 256), f32),
            pltpu.VMEM((128, 128), f32),
            pltpu.VMEM((128, 128), f32),
        ]
        + [pltpu.VMEM((256, WINDOW), jnp.bfloat16)] * 16
        + [dma, dma, dma((2,)), dma((2,)), dma((2,)), dma((2,)), dma((2,))],
        compiler_params=pltpu.CompilerParams(
            collective_id=0, has_side_effects=True, vmem_limit_bytes=60 * 2**20
        ),
        name="match",
    )(
        raw.T,
        stencil,
        mad.reshape(1, CHAN),
        templates,
        shifts.reshape(-1),
        listed,
        counts,
    )
    return total / jnp.sqrt(jnp.maximum(tally, 1.0) * CHAN)


def solution(mesh):
    in_specs = (
        P("sec", None),
        P(),
        P("sec"),
        P(("sec", "tpl"), None),
        P(None, "sec"),
        P("sec", "tpl"),
        P("sec", "tpl"),
    )
    out_specs = P(("sec", "tpl"), None)
    return jax.shard_map(shards, mesh=mesh, in_specs=in_specs, out_specs=out_specs, check_vma=False)
```

time: 229 us -> 43.1 us (0.19)
  local copies, waits for them, and re-layouts: 87.8 us -> 1.27 us
  Pallas kernels: 0 us -> 39.6 us
  waiting for transfers between devices: 38.1 us -> 0 us
  matrix products: 36 us -> 0 us
  other arithmetic: 26.6 us -> 1.32 us
  starting transfers between devices: 24.2 us -> 0 us
  between operations: 14.2 us -> 0.66 us
    gather x128 -> x0, local copies, waits for them, and re-layouts: 65.1 us -> none
    pallas_call x0 -> x1, Pallas kernels: none -> 39.6 us  [shards(): pl.pallas_call(kernel, out_shape=(out, out), in_specs=[pl.BlockSpec(memor...]
    dot_general x11 -> x0, matrix products: 36 us -> none  [the longest x8 32.2 us: one_block(): jnp.einsum('mci,kti->mckt', segments, matrix, preferred_element_type=jnp....]
    convert_element_type x1 -> x0, other arithmetic: 21.5 us -> none  [shards(): whitened = (filtered / mad[:, None]).astype(jnp.bfloat16)]
    all_gather x1 -> x0, waiting for transfers between devices: 19.8 us -> none  [shards(): piece = lax.all_gather(templates, ('sec', 'tpl'), axis=0, tiled=True)]
    all_to_all x2 -> x0, waiting for transfers between devices: 18.2 us -> none  [the longest x1 9.59 us: shards(): lax.all_to_all(send_rows, ('sec', 'tpl'), split_axis=0, concat_axis=0, ti...]
    all_to_all x2 -> x0, starting transfers between devices: 17.4 us -> none  [the longest x1 12.1 us: shards(): lax.all_to_all(wanted.reshape(devices, PER_OWNER), ('sec', 'tpl'), split_...]
    reshape x10 -> x1, local copies, waits for them, and re-layouts: 11.9 us -> 1.27 us  [shards(): mad.reshape(1, CHAN)]
  transfers between devices with their start and end apart: 5 -> 0, of which waited for: 3 -> 0; matrix products, arithmetic and copies ran while one was open for 12% -> 0% of each run, Pallas kernels for 0% -> 0%
where the time goes in v1:
time: 43.1 us; the launch traced here: 42.8 us
  Pallas kernels  39.6 us (92%)
  other arithmetic  1.32 us (3%)
  local copies, waits for them, and re-layouts  1.27 us (3%)
  between operations  0.66 us (2%)
    pallas_call x1, Pallas kernels, shards(): pl.pallas_call(kernel, out_shape=(out, out), in_specs=[pl.BlockSpec(memor...  39.6 us
    div x1, other arithmetic, shards(): return total / jnp.sqrt(jnp.maximum(tally, 1.0) * CHAN)  1.32 us
    reshape x1, local copies, waits for them, and re-layouts, shards(): mad.reshape(1, CHAN)  1.27 us

profile of v1, /device:TPU:1, one launch (start us, length us, event | category | flops | bytes accessed | tf_op | source)
XLA Modules:
  0.0 42.8 jit_solution(3619439948373017007)
XLA Ops:
  0.7 1.3 %reshape.6.mad_ref = f32[1,768]{1,0:T(1,128)} reshape(f32[768]{0:T(1024)} %param.9) | data formatting | bytes 6144 | tf_op jit(solution)/shard_map/reshape | solution.py:316
  1.9 39.6 %match.1 = (f32[16,128]{1,0:T(8,128)}, f32[16,128]{1,0:T(8,128)}) custom-call(f32[899,768]{1,0:T(8,128)} %bitcast.2, f32[3,5]{1,0:T(4,128)} %stencil_ref.1, f32[1,768]{1,0:T(1,128)} %reshape.6.mad_ref, bf16[16,512]{1,0:T(8,128)(2,1)} %templates_ref.1, s32[2048]{0:T(1024)} %bitcast.3, s32[1,32]{1,0:T(1,128)} %listed_ref.1, s32[1,1]{1,0:T(1,128)S(6)} %copy.8.counts_ref), custom_call_target="tpu_custom_call" | custom-call | tf_op jit(solution)/shard_map/match/pallas_call | solution.py:285
  41.5 1.3 %rsqrt_multiply_fusion = f32[16,128]{1,0:T(8,128)} fusion(f32[16,128]{1,0:T(8,128)} %get-tuple-element.7, f32[16,128]{1,0:T(8,128)} %get-tuple-element.8), kind=kLoop, calls=%fused_computation | loop fusion | flops 6144 | bytes 24576 | tf_op jit(solution)/shard_map/div | solution.py:322

commit v2 on v1

v2 whole, which is shorter than its diff:
```python
import functools

import jax
import jax.numpy as jnp
from jax import lax
from jax.experimental import pallas as pl
from jax.experimental.pallas import tpu as pltpu
from jax.sharding import PartitionSpec as P

MESH = pl.DeviceIdType.MESH
DEVICES = 128
CHAN = 768
LAGS = 128
TLEN = 512
SLOTS = 32
OWN = 16
WINDOW = 768
WIDTH = 896
PAIRS = SLOTS // 2 + 1
NBANDS = 16
LEAD = 8
ROWS = 16
UNROLL = 4
TILES = WIDTH // 128
CUTS = (4, 6)
NT = (((1,), (1,)), ((), ()))
TN = (((0,), (0,)), ((), ()))


def hops(step):
    return sum((0, 1, 2, 1)[d] for d in step[:3])


STEPS = sorted(
    [
        (dz, dy, dx, dc)
        for dz in range(4)
        for dy in range(4)
        for dx in range(4)
        for dc in range(2)
    ],
    key=lambda step: (hops(step), step),
    reverse=True,
)
BACK = [
    STEPS.index(((4 - dz) % 4, (4 - dy) % 4, (4 - dx) % 4, dc)) for dz, dy, dx, dc in STEPS
]
SELF = DEVICES - 1
MID = sum(hops(step) >= 3 for step in STEPS)
GROUPS = ((MID, DEVICES), (0, MID))


def peers():
    sec = lax.axis_index("sec")
    tpl = lax.axis_index("tpl")
    z = sec // 8
    y = sec // 2 % 4
    x = sec % 2 * 2 + tpl // 2
    core = tpl % 2
    zs = [(z + d) % 4 * 8 for d in range(4)]
    ys = [(y + d) % 4 * 2 for d in range(4)]
    xs = [(x + d) % 4 for d in range(4)]
    his = [v // 2 for v in xs]
    los = [v % 2 * 2 for v in xs]
    cores = [(core + d) % 2 for d in range(2)]
    out = []
    for dz, dy, dx, dc in STEPS:
        s = zs[dz] + ys[dy] + his[dx]
        t = los[dx] + cores[dc]
        out.append((s, t))
    return sec, tpl, out


def robust(value):
    return value * lax.rsqrt(1.0 + value * value)


def build(rows, shift):
    flat = jnp.concatenate(
        [jnp.broadcast_to(rows[k : k + 1], (8, 128)) for k in range(4)]
        + [jnp.zeros((8, WINDOW - TLEN), jnp.float32)],
        axis=1,
    )
    base = pltpu.roll(flat, shift, 1)
    base = pltpu.roll(base, 0, 1, stride=1, stride_axis=0)
    both = jnp.concatenate([base, pltpu.roll(base, 8, 1)], axis=0).astype(jnp.bfloat16)
    return jnp.concatenate([pltpu.roll(both, 16 * g, 1) if g else both for g in range(8)], axis=0)


def split3(value):
    high = value.astype(jnp.bfloat16)
    left = value - high.astype(jnp.float32)
    middle = left.astype(jnp.bfloat16)
    low = (left - middle.astype(jnp.float32)).astype(jnp.bfloat16)
    return [high, middle, low]


def kernel(
    raw_hbm,
    stencil_hbm,
    mad_hbm,
    templates_hbm,
    shifts_hbm,
    listed_hbm,
    counts_hbm,
    total_ref,
    tally_ref,
    raw_v,
    stencil_ref,
    mad_ref,
    templates_ref,
    shifts_ref,
    listed_ref,
    counts_ref,
    tile_v,
    edge_v,
    halo_out,
    halo_in,
    white,
    inv_mad,
    name_out,
    name_in,
    row_out,
    row_in,
    part_out,
    part_in,
    info_v,
    info_s,
    acc,
    pick_v,
    *rest,
):
    bands = rest[:NBANDS]
    load_sems, info_sem, halo_send, halo_recv, name_sems, row_sems, part_sems = rest[NBANDS:]
    sec, tpl, others = peers()

    barrier = pltpu.get_barrier_semaphore()
    loads = [
        pltpu.make_async_copy(src, dst, load_sems.at[k])
        for k, (src, dst) in enumerate(
            [
                (listed_hbm, listed_ref),
                (counts_hbm, counts_ref),
                (shifts_hbm, shifts_ref),
                (stencil_hbm, stencil_ref),
                (mad_hbm, mad_ref),
                (templates_hbm, templates_ref),
            ]
            + [(raw_hbm.at[:, pl.ds(128 * k, 128)], raw_v.at[k, pl.ds(0, 899)]) for k in range(CHAN // 128)]
        )
    ]
    for copy in loads[:3]:
        copy.start()
    for s, t in others[:SELF]:
        pl.semaphore_signal(barrier, inc=1, device_id=(s, t), device_id_type=MESH)
    for copy in loads[3:]:
        copy.start()

    def send(src, dst, i, to, send_sem, recv_sem):
        s, t = others[to]
        pltpu.make_async_remote_copy(
            src_ref=src.at[i],
            dst_ref=dst.at[i],
            send_sem=send_sem,
            recv_sem=recv_sem,
            device_id=(s, t),
            device_id_type=MESH,
        ).start()

    def keep(src, dst, recv_sem):
        pltpu.make_async_copy(src.at[SELF], dst.at[SELF], recv_sem).start()

    def got(src, dst, lo, hi, recv_sem):
        part = pl.ds(lo, hi - lo)
        pltpu.make_async_copy(src.at[part], dst.at[part], recv_sem).wait()

    loads[0].wait()
    loads[1].wait()
    loads[2].wait()
    lane = lax.broadcasted_iota(jnp.int32, (SLOTS, 128), 1)
    slot = lax.broadcasted_iota(jnp.int32, (SLOTS, 128), 0)
    lane_row = lax.broadcasted_iota(jnp.int32, (8, 128), 1)
    ids = jnp.zeros((8, 128), jnp.int32)
    for i, (s, t) in enumerate(others):
        ids = jnp.where(lane_row == i, s * 4 + t, ids)
    ids = jnp.concatenate([ids] * (SLOTS // 8), axis=0)
    name = jnp.zeros((SLOTS, 128), jnp.int32)
    rest_shift = jnp.zeros((SLOTS, 128), jnp.int32)
    place = jnp.zeros((SLOTS, 128), jnp.int32)
    early_slots = jnp.int32(0)
    for q in range(SLOTS):
        k = listed_ref[0, q]
        moved = shifts_ref[k]
        late = (moved >= 128).astype(jnp.int32)
        spot = early_slots + late * (2 * PAIRS - 1 - q)
        early_slots = early_slots + 1 - late
        name = jnp.where(slot == q, k, name)
        rest_shift = jnp.where(slot == q, moved - 128 * late, rest_shift)
        place = jnp.where(slot == q, spot, place)
    owner = name // OWN
    within = name - owner * OWN
    live = slot < counts_ref[0, 0]
    owned = owner == ids
    own_hot = owned.astype(jnp.bfloat16)
    asked = jnp.where(live, within + 1, 0).astype(jnp.bfloat16)
    name_out[:, 0, :] = lax.dot_general(own_hot, asked, TN, preferred_element_type=jnp.float32)

    pl.semaphore_wait(barrier, DEVICES - 1)
    for g in (1, 0):
        for i in range(*GROUPS[g]):
            if i < SELF:
                send(name_out, name_in, i, i, name_sems.at[3], name_sems.at[g])
    keep(name_out, name_in, name_sems.at[0])
    loads[5].wait()
    loads[3].wait()
    loads[4].wait()
    inv_mad[...] = jnp.broadcast_to((1.0 / mad_ref[...]).reshape(1, CHAN), (8, CHAN))
    for copy in loads[6:]:
        copy.wait()
    raw_v[:, 899:, :] = jnp.zeros((CHAN // 128, 5, 128), jnp.float32)
    chunks = CHAN // 128
    lane_block = lax.broadcasted_iota(jnp.int32, (ROWS, 128), 1)
    nothing = jnp.zeros((ROWS, 128), jnp.float32)

    def whiten_rows(start, base):
        across = [[], [], []]
        for k in range(chunks):
            taps = [raw_v[k, pl.ds(start + base + b, ROWS), :] for b in range(5)]
            for a in range(3):
                value = stencil_ref[a, 0] * taps[0]
                for b in range(1, 5):
                    value = value + stencil_ref[a, b] * taps[b]
                across[a].append(value)
        lower = [pltpu.roll(value, 1, 1) for value in across[0]]
        upper = [pltpu.roll(value, 127, 1) for value in across[2]]
        for k in range(chunks):
            left = jnp.where(lane_block == 0, lower[k - 1] if k else nothing, lower[k])
            right = jnp.where(
                lane_block == 127, upper[k + 1] if k < chunks - 1 else nothing, upper[k]
            )
            done = (across[1][k] + left + right) * inv_mad[0:1, 128 * k : 128 * k + 128]
            tile_v[pl.ds(base, ROWS), 128 * k : 128 * k + 128] = done

    def whiten(lo, hi):
        for t in range(lo, hi):

            def step(i, carry):
                for k in range(UNROLL):
                    whiten_rows(128 * t, pl.multiple_of((i * UNROLL + k) * ROWS, ROWS))
                return carry

            lax.fori_loop(0, 128 // ROWS // UNROLL, step, 0)
            here = slice(128 * t, 128 * t + 128)
            done = tile_v[:, :CHAN].T
            edge_v[0, :, here] = done[:16]
            edge_v[1, :, here] = done[CHAN - 16 :]
            done = done.astype(jnp.bfloat16)
            if t < TILES - 1:
                white[0, :, here] = done
            if t > 0:
                white[1, :, 128 * t - 128 : 128 * t] = done

    def halo(t):
        for side, k, a in ((0, chunks - 1, 0), (1, 0, 2)):
            value = stencil_ref[a, 0] * raw_v[k, 128 * t : 128 * t + 128, :]
            for b in range(1, 5):
                value = value + stencil_ref[a, b] * raw_v[k, 128 * t + b : 128 * t + b + 128, :]
            turned = value.T
            halo_out[side, :, 128 * t : 128 * t + 128] = turned[:8] if side else turned[120:]

    for t in range(TILES):
        halo(t)
    up = pltpu.make_async_remote_copy(
        src_ref=halo_out.at[0],
        dst_ref=halo_in.at[0],
        send_sem=halo_send.at[0],
        recv_sem=halo_recv.at[0],
        device_id=((sec + 1) % 32, tpl),
        device_id_type=MESH,
    )
    down = pltpu.make_async_remote_copy(
        src_ref=halo_out.at[1],
        dst_ref=halo_in.at[1],
        send_sem=halo_send.at[1],
        recv_sem=halo_recv.at[1],
        device_id=((sec + 31) % 32, tpl),
        device_id_type=MESH,
    )
    up.start()
    down.start()

    hot = place == lane
    index = jnp.sum(jnp.where(owned, lane, 0), axis=1, keepdims=True)
    info_v[0:1, :] = jnp.sum(jnp.where(hot, rest_shift, 0), axis=0, keepdims=True)
    info_v[1:2, :] = jnp.sum(jnp.where(hot, index, 0), axis=0, keepdims=True)
    info_v[2:8, :] = jnp.zeros((6, 128), jnp.int32)
    info = pltpu.make_async_copy(info_v, info_s, info_sem)
    info.start()
    even_hot = (place == 2 * lane).astype(jnp.bfloat16)
    odd_hot = (place == 2 * lane + 1).astype(jnp.bfloat16)
    even = lax.dot_general(even_hot, own_hot, TN, preferred_element_type=jnp.float32)[:32]
    odd = lax.dot_general(odd_hot, own_hot, TN, preferred_element_type=jnp.float32)[:32]
    pick_v[...] = jnp.concatenate([even] * 3 + [odd] * 3, axis=0).astype(jnp.bfloat16)
    acc[...] = jnp.zeros_like(acc)

    def answer(g):
        lo, hi = GROUPS[g]
        got(name_out, name_in, lo, hi, name_sems.at[g])
        wanted = name_in[lo:hi, 0, :]
        lanes = lax.broadcasted_iota(jnp.int32, (hi - lo, 128), 1)
        into = jnp.where(wanted == (lanes + 1).astype(jnp.float32), 1.0, 0.0).astype(jnp.bfloat16)
        chosen = jnp.dot(into[:, :OWN], templates_ref[...], preferred_element_type=jnp.float32)
        for k in range(4):
            row_out[lo:hi, k, :] = chosen[:, 128 * k : 128 * k + 128]
        for i in range(lo, hi):
            if i < SELF:
                send(row_out, row_in, i, BACK[i], row_sems.at[0], row_sems.at[1])
        if hi == DEVICES:
            keep(row_out, row_in, row_sems.at[1])

    whiten(0, CUTS[0])
    answer(0)
    whiten(CUTS[0], CUTS[1])
    answer(1)
    whiten(CUTS[1], TILES)

    lanes = lax.broadcasted_iota(jnp.int32, (DEVICES, 128), 1)
    into = jnp.where(name_in[:, 0, :] == (lanes + 1).astype(jnp.float32), 1.0, 0.0)
    into = into.astype(jnp.bfloat16)
    ones = jnp.ones((DEVICES, 128), jnp.bfloat16)
    tally = lax.dot_general(into, ones, TN, preferred_element_type=jnp.float32)
    tally_ref[...] = tally[:OWN]

    up.wait()
    down.wait()
    edge_row = lax.broadcasted_iota(jnp.int32, (16, WIDTH), 0)
    for side, row, end, channel, start in ((0, 7, 0, 0, 0), (1, 0, 31, CHAN - 1, CHAN - 16)):
        extra = halo_in[side, row : row + 1, :] * inv_mad[0:1, channel : channel + 1]
        hit = (edge_row == channel - start) & (sec != end)
        done = (edge_v[side] + jnp.where(hit, extra, 0.0)).astype(jnp.bfloat16)
        white[0, start : start + 16, :] = done[:, :WINDOW]
        white[1, start : start + 16, :] = done[:, 128:]

    info.wait()
    got(row_out, row_in, 0, DEVICES, row_sems.at[1])

    def prepare(j, band):
        for h in range(2):
            rows = row_in[info_s[1, 2 * j + h]]
            band[128 * h : 128 * h + 128, :] = build(rows, info_s[0, 2 * j + h])

    def correlate(j, band):
        half = (2 * j >= early_slots).astype(jnp.int32)
        corr = lax.dot_general(white[half], band[...], NT, preferred_element_type=jnp.float32)
        acc[j] = robust(corr).reshape(CHAN // 8, 8, 256).sum(axis=0)

    for u in range(LEAD):
        prepare(u, bands[u])
    for u in range(PAIRS):
        if u + LEAD < PAIRS:
            prepare(u + LEAD, bands[(u + LEAD) % NBANDS])
        correlate(u, bands[u % NBANDS])

    sums = jnp.sum(acc[...], axis=1)
    parts = jnp.concatenate(split3(sums[:, :128]) + split3(sums[:, 128:]), axis=0)
    part_out[:, 0, :] = lax.dot_general(pick_v[...], parts, TN, preferred_element_type=jnp.float32)
    for i in range(SELF):
        send(part_out, part_in, i, i, part_sems.at[0], part_sems.at[1])
    keep(part_out, part_in, part_sems.at[1])
    into = jnp.concatenate([into] * 3, axis=0)
    got(name_out, name_in, 0, SELF, name_sems.at[3])
    got(row_out, row_in, 0, SELF, row_sems.at[0])
    got(part_out, part_in, 0, DEVICES, part_sems.at[1])
    arrived = jnp.concatenate(split3(part_in[:, 0, :]), axis=0)
    total = lax.dot_general(into, arrived, TN, preferred_element_type=jnp.float32)
    total_ref[...] = total[:OWN]
    got(part_out, part_in, 0, SELF, part_sems.at[0])


def shards(raw, stencil, mad, templates, shifts, listed, counts):
    vmem = pl.BlockSpec(memory_space=pltpu.VMEM)
    hbm = pl.BlockSpec(memory_space=pl.ANY)
    f32 = jnp.float32
    dma = pltpu.SemaphoreType.DMA
    out = jax.ShapeDtypeStruct((OWN, LAGS), f32)
    total, tally = pl.pallas_call(
        kernel,
        out_shape=(out, out),
        in_specs=[hbm] * 7,
        out_specs=(vmem, vmem),
        scratch_shapes=[
            pltpu.VMEM((CHAN // 128, 904, 128), f32),
            pltpu.SMEM((3, 5), f32),
            pltpu.VMEM((CHAN,), f32),
            pltpu.VMEM((OWN, TLEN), jnp.bfloat16),
            pltpu.SMEM((2048,), jnp.int32),
            pltpu.SMEM((1, SLOTS), jnp.int32),
            pltpu.SMEM((1, 1), jnp.int32),
            pltpu.VMEM((128, CHAN), f32),
            pltpu.VMEM((2, 16, WIDTH), f32),
            pltpu.VMEM((2, 8, WIDTH), f32),
            pltpu.VMEM((2, 8, WIDTH), f32),
            pltpu.VMEM((2, CHAN, WINDOW), jnp.bfloat16),
            pltpu.VMEM((8, CHAN), f32),
            pltpu.VMEM((DEVICES, 1, 128), f32),
            pltpu.VMEM((DEVICES, 1, 128), f32),
            pltpu.VMEM((DEVICES, 4, 128), f32),
            pltpu.VMEM((DEVICES, 4, 128), f32),
            pltpu.VMEM((DEVICES, 1, 128), f32),
            pltpu.VMEM((DEVICES, 1, 128), f32),
            pltpu.VMEM((8, 128), jnp.int32),
            pltpu.SMEM((8, 128), jnp.int32),
            pltpu.VMEM((32, 8, 256), f32),
            pltpu.VMEM((6 * 32, 128), jnp.bfloat16),
        ]
        + [pltpu.VMEM((256, WINDOW), jnp.bfloat16)] * NBANDS
        + [dma((12,)), dma, dma((2,)), dma((2,)), dma((4,)), dma((2,)), dma((2,))],
        compiler_params=pltpu.CompilerParams(
            collective_id=0, has_side_effects=True, vmem_limit_bytes=60 * 2**20
        ),
        name="match",
    )(raw.T, stencil, mad, templates, shifts.reshape(-1), listed, counts)
    return total / jnp.sqrt(jnp.maximum(tally, 1.0) * CHAN)


def solution(mesh):
    in_specs = (
        P("sec", None),
        P(),
        P("sec"),
        P(("sec", "tpl"), None),
        P(None, "sec"),
        P("sec", "tpl"),
        P("sec", "tpl"),
    )
    out_specs = P(("sec", "tpl"), None)
    return jax.shard_map(shards, mesh=mesh, in_specs=in_specs, out_specs=out_specs, check_vma=False)
```

time: 43.1 us -> 39 us (0.905)
  Pallas kernels: 39.6 us -> 36.9 us
  local copies, waits for them, and re-layouts: 1.27 us -> 0 us
    pallas_call x1, Pallas kernels: 39.6 us -> 36.9 us  [shards(): pl.pallas_call(kernel, out_shape=(out, out), in_specs=[hbm] * 7, out_spec...]
    reshape x1 -> x0, local copies, waits for them, and re-layouts: 1.27 us -> none  [shards(): mad.reshape(1, CHAN)]
where the time goes in v2:
time: 39 us; the launch traced here: 38.8 us
  Pallas kernels  36.9 us (95%)
  other arithmetic  1.32 us (3%)
  between operations  0.66 us (2%)
    pallas_call x1, Pallas kernels, shards(): pl.pallas_call(kernel, out_shape=(out, out), in_specs=[hbm] * 7, out_spec...  36.9 us
    div x1, other arithmetic, shards(): return total / jnp.sqrt(jnp.maximum(tally, 1.0) * CHAN)  1.32 us

profile of v2, /device:TPU:1, one launch (start us, length us, event | category | flops | bytes accessed | tf_op | source)
XLA Modules:
  0.0 38.8 jit_solution(12342964949308034900)
XLA Ops:
  0.7 36.9 %match.1 = (f32[16,128]{1,0:T(8,128)}, f32[16,128]{1,0:T(8,128)}) custom-call(f32[899,768]{1,0:T(8,128)} %bitcast.2, f32[3,5]{1,0:T(4,128)} %stencil_hbm.1, f32[768]{0:T(1024)} %mad_hbm.1, bf16[16,512]{1,0:T(8,128)(2,1)} %templates_hbm.1, s32[2048]{0:T(1024)} %bitcast.3, s32[1,32]{1,0:T(1,128)} %listed_hbm.1, s32[1,1]{1,0:T(1,128)S(6)} %copy.8.counts_hbm), custom_call_target="tpu_custom_call" | custom-call | tf_op jit(solution)/shard_map/match/pallas_call | solution.py:386
  37.5 1.3 %rsqrt_multiply_fusion = f32[16,128]{1,0:T(8,128)} fusion(f32[16,128]{1,0:T(8,128)} %get-tuple-element.7, f32[16,128]{1,0:T(8,128)} %get-tuple-element.8), kind=kLoop, calls=%fused_computation | loop fusion | flops 6144 | bytes 24576 | tf_op jit(solution)/shard_map/div | solution.py:423

commit v3 on v2

--- a/solution.py
+++ b/solution.py
@@ -22,7 +22,7 @@
 ROWS = 16
 UNROLL = 4
 TILES = WIDTH // 128
-CUTS = (4, 6)
+CUTS = (4,)
 NT = (((1,), (1,)), ((), ()))
 TN = (((0,), (0,)), ((), ()))
 
@@ -46,8 +46,7 @@
     STEPS.index(((4 - dz) % 4, (4 - dy) % 4, (4 - dx) % 4, dc)) for dz, dy, dx, dc in STEPS
 ]
 SELF = DEVICES - 1
-MID = sum(hops(step) >= 3 for step in STEPS)
-GROUPS = ((MID, DEVICES), (0, MID))
+GROUPS = ((0, DEVICES),)
 
 
 def peers():
@@ -206,7 +205,7 @@
     name_out[:, 0, :] = lax.dot_general(own_hot, asked, TN, preferred_element_type=jnp.float32)
 
     pl.semaphore_wait(barrier, DEVICES - 1)
-    for g in (1, 0):
+    for g in (0,):
         for i in range(*GROUPS[g]):
             if i < SELF:
                 send(name_out, name_in, i, i, name_sems.at[3], name_sems.at[g])
@@ -310,8 +309,7 @@
         lanes = lax.broadcasted_iota(jnp.int32, (hi - lo, 128), 1)
         into = jnp.where(wanted == (lanes + 1).astype(jnp.float32), 1.0, 0.0).astype(jnp.bfloat16)
         chosen = jnp.dot(into[:, :OWN], templates_ref[...], preferred_element_type=jnp.float32)
-        for k in range(4):
-            row_out[lo:hi, k, :] = chosen[:, 128 * k : 128 * k + 128]
+        row_out[lo:hi] = chosen.reshape(hi - lo, 4, 128).astype(jnp.bfloat16)
         for i in range(lo, hi):
             if i < SELF:
                 send(row_out, row_in, i, BACK[i], row_sems.at[0], row_sems.at[1])
@@ -320,9 +318,7 @@
 
     whiten(0, CUTS[0])
     answer(0)
-    whiten(CUTS[0], CUTS[1])
-    answer(1)
-    whiten(CUTS[1], TILES)
+    whiten(CUTS[0], TILES)
 
     lanes = lax.broadcasted_iota(jnp.int32, (DEVICES, 128), 1)
     into = jnp.where(name_in[:, 0, :] == (lanes + 1).astype(jnp.float32), 1.0, 0.0)
@@ -346,7 +342,7 @@
 
     def prepare(j, band):
         for h in range(2):
-            rows = row_in[info_s[1, 2 * j + h]]
+            rows = row_in[info_s[1, 2 * j + h]].astype(jnp.float32)
             band[128 * h : 128 * h + 128, :] = build(rows, info_s[0, 2 * j + h])
 
     def correlate(j, band):
@@ -404,8 +400,8 @@
             pltpu.VMEM((8, CHAN), f32),
             pltpu.VMEM((DEVICES, 1, 128), f32),
             pltpu.VMEM((DEVICES, 1, 128), f32),
-            pltpu.VMEM((DEVICES, 4, 128), f32),
-            pltpu.VMEM((DEVICES, 4, 128), f32),
+            pltpu.VMEM((DEVICES, 4, 128), jnp.bfloat16),
+            pltpu.VMEM((DEVICES, 4, 128), jnp.bfloat16),
             pltpu.VMEM((DEVICES, 1, 128), f32),
             pltpu.VMEM((DEVICES, 1, 128), f32),
             pltpu.VMEM((8, 128), jnp.int32),

time: 39 us -> 37.7 us (0.967)
  Pallas kernels: 36.9 us -> 35.5 us
    pallas_call x1, Pallas kernels: 36.9 us -> 35.5 us  [shards(): pl.pallas_call(kernel, out_shape=(out, out), in_specs=[hbm] * 7, out_spec...]
where the time goes in v3:
time: 37.7 us; the launch traced here: 37.5 us
  Pallas kernels  35.5 us (94%)
  other arithmetic  1.32 us (4%)
  between operations  0.66 us (2%)
    pallas_call x1, Pallas kernels, shards(): pl.pallas_call(kernel, out_shape=(out, out), in_specs=[hbm] * 7, out_spec...  35.5 us
    div x1, other arithmetic, shards(): return total / jnp.sqrt(jnp.maximum(tally, 1.0) * CHAN)  1.32 us

profile of v3, /device:TPU:1, one launch (start us, length us, event | category | flops | bytes accessed | tf_op | source)
XLA Modules:
  0.0 37.5 jit_solution(5621409138340328058)
XLA Ops:
  0.7 35.5 %match.1 = (f32[16,128]{1,0:T(8,128)}, f32[16,128]{1,0:T(8,128)}) custom-call(f32[899,768]{1,0:T(8,128)} %bitcast.2, f32[3,5]{1,0:T(4,128)} %stencil_hbm.1, f32[768]{0:T(1024)} %mad_hbm.1, bf16[16,512]{1,0:T(8,128)(2,1)} %templates_hbm.1, s32[2048]{0:T(1024)} %bitcast.3, s32[1,32]{1,0:T(1,128)} %listed_hbm.1, s32[1,1]{1,0:T(1,128)S(6)} %copy.8.counts_hbm), custom_call_target="tpu_custom_call" | custom-call | tf_op jit(solution)/shard_map/match/pallas_call | solution.py:382
  36.2 1.3 %rsqrt_multiply_fusion = f32[16,128]{1,0:T(8,128)} fusion(f32[16,128]{1,0:T(8,128)} %get-tuple-element.7, f32[16,128]{1,0:T(8,128)} %get-tuple-element.8), kind=kLoop, calls=%fused_computation | loop fusion | flops 6144 | bytes 24576 | tf_op jit(solution)/shard_map/div | solution.py:419

commit v4 on v3

--- a/solution.py
+++ b/solution.py
@@ -82,8 +82,9 @@
     )
     base = pltpu.roll(flat, shift, 1)
     base = pltpu.roll(base, 0, 1, stride=1, stride_axis=0)
-    both = jnp.concatenate([base, pltpu.roll(base, 8, 1)], axis=0).astype(jnp.bfloat16)
-    return jnp.concatenate([pltpu.roll(both, 16 * g, 1) if g else both for g in range(8)], axis=0)
+    return jnp.concatenate(
+        [pltpu.roll(base, 8 * g, 1) if g else base for g in range(16)], axis=0
+    ).astype(jnp.bfloat16)
 
 
 def split3(value):

time: 37.7 us -> 36.8 us (0.976)
  Pallas kernels: 35.5 us -> 34.6 us
    pallas_call x1, Pallas kernels: 35.5 us -> 34.6 us  [shards(): pl.pallas_call(kernel, out_shape=(out, out), in_specs=[hbm] * 7, out_spec...]
where the time goes in v4:
time: 36.8 us; the launch traced here: 36.6 us
  Pallas kernels  34.6 us (94%)
  other arithmetic  1.32 us (4%)
  between operations  0.66 us (2%)
    pallas_call x1, Pallas kernels, shards(): pl.pallas_call(kernel, out_shape=(out, out), in_specs=[hbm] * 7, out_spec...  34.6 us
    div x1, other arithmetic, shards(): return total / jnp.sqrt(jnp.maximum(tally, 1.0) * CHAN)  1.32 us

profile of v4, /device:TPU:1, one launch (start us, length us, event | category | flops | bytes accessed | tf_op | source)
XLA Modules:
  0.0 36.6 jit_solution(8007675778132765993)
XLA Ops:
  0.7 34.6 %match.1 = (f32[16,128]{1,0:T(8,128)}, f32[16,128]{1,0:T(8,128)}) custom-call(f32[899,768]{1,0:T(8,128)} %bitcast.2, f32[3,5]{1,0:T(4,128)} %stencil_hbm.1, f32[768]{0:T(1024)} %mad_hbm.1, bf16[16,512]{1,0:T(8,128)(2,1)} %templates_hbm.1, s32[2048]{0:T(1024)} %bitcast.3, s32[1,32]{1,0:T(1,128)} %listed_hbm.1, s32[1,1]{1,0:T(1,128)S(6)} %copy.8.counts_hbm), custom_call_target="tpu_custom_call" | custom-call | tf_op jit(solution)/shard_map/match/pallas_call | solution.py:383
  35.3 1.3 %rsqrt_multiply_fusion = f32[16,128]{1,0:T(8,128)} fusion(f32[16,128]{1,0:T(8,128)} %get-tuple-element.7, f32[16,128]{1,0:T(8,128)} %get-tuple-element.8), kind=kLoop, calls=%fused_computation | loop fusion | flops 6144 | bytes 24576 | tf_op jit(solution)/shard_map/div | solution.py:420

commit v5 on v3

--- a/solution.py
+++ b/solution.py
@@ -17,8 +17,8 @@
 WINDOW = 768
 WIDTH = 896
 PAIRS = SLOTS // 2 + 1
-NBANDS = 16
-LEAD = 8
+NBANDS = 17
+LEAD = 2
 ROWS = 16
 UNROLL = 4
 TILES = WIDTH // 128
@@ -74,7 +74,7 @@
     return value * lax.rsqrt(1.0 + value * value)
 
 
-def build(rows, shift):
+def build(band, at, rows, shift):
     flat = jnp.concatenate(
         [jnp.broadcast_to(rows[k : k + 1], (8, 128)) for k in range(4)]
         + [jnp.zeros((8, WINDOW - TLEN), jnp.float32)],
@@ -82,8 +82,9 @@
     )
     base = pltpu.roll(flat, shift, 1)
     base = pltpu.roll(base, 0, 1, stride=1, stride_axis=0)
-    both = jnp.concatenate([base, pltpu.roll(base, 8, 1)], axis=0).astype(jnp.bfloat16)
-    return jnp.concatenate([pltpu.roll(both, 16 * g, 1) if g else both for g in range(8)], axis=0)
+    for g in range(8):
+        pair = [pltpu.roll(base, 8 * k, 1) if k else base for k in (2 * g, 2 * g + 1)]
+        band[at + 16 * g : at + 16 * g + 16, :] = jnp.concatenate(pair, axis=0).astype(jnp.bfloat16)
 
 
 def split3(value):
@@ -343,7 +344,7 @@
     def prepare(j, band):
         for h in range(2):
             rows = row_in[info_s[1, 2 * j + h]].astype(jnp.float32)
-            band[128 * h : 128 * h + 128, :] = build(rows, info_s[0, 2 * j + h])
+            build(band, 128 * h, rows, info_s[0, 2 * j + h])
 
     def correlate(j, band):
         half = (2 * j >= early_slots).astype(jnp.int32)

time: 37.7 us -> 36.8 us (0.976)
  Pallas kernels: 35.5 us -> 34.6 us
    pallas_call x1, Pallas kernels: 35.5 us -> 34.6 us  [shards(): pl.pallas_call(kernel, out_shape=(out, out), in_specs=[hbm] * 7, out_spec...]
where the time goes in v5:
time: 36.8 us; the launch traced here: 36.6 us
  Pallas kernels  34.6 us (94%)
  other arithmetic  1.32 us (4%)
  between operations  0.66 us (2%)
    pallas_call x1, Pallas kernels, shards(): pl.pallas_call(kernel, out_shape=(out, out), in_specs=[hbm] * 7, out_spec...  34.6 us
    div x1, other arithmetic, shards(): return total / jnp.sqrt(jnp.maximum(tally, 1.0) * CHAN)  1.32 us

profile of v5, /device:TPU:1, one launch (start us, length us, event | category | flops | bytes accessed | tf_op | source)
XLA Modules:
  0.0 36.6 jit_solution(8007675778132765993)
XLA Ops:
  0.7 34.6 %match.1 = (f32[16,128]{1,0:T(8,128)}, f32[16,128]{1,0:T(8,128)}) custom-call(f32[899,768]{1,0:T(8,128)} %bitcast.2, f32[3,5]{1,0:T(4,128)} %stencil_hbm.1, f32[768]{0:T(1024)} %mad_hbm.1, bf16[16,512]{1,0:T(8,128)(2,1)} %templates_hbm.1, s32[2048]{0:T(1024)} %bitcast.3, s32[1,32]{1,0:T(1,128)} %listed_hbm.1, s32[1,1]{1,0:T(1,128)S(6)} %copy.8.counts_hbm), custom_call_target="tpu_custom_call" | custom-call | tf_op jit(solution)/shard_map/match/pallas_call | solution.py:383
  35.3 1.3 %rsqrt_multiply_fusion = f32[16,128]{1,0:T(8,128)} fusion(f32[16,128]{1,0:T(8,128)} %get-tuple-element.7, f32[16,128]{1,0:T(8,128)} %get-tuple-element.8), kind=kLoop, calls=%fused_computation | loop fusion | flops 6144 | bytes 24576 | tf_op jit(solution)/shard_map/div | solution.py:420

commit v6 on v5

--- a/solution.py
+++ b/solution.py
@@ -300,7 +300,7 @@
     odd_hot = (place == 2 * lane + 1).astype(jnp.bfloat16)
     even = lax.dot_general(even_hot, own_hot, TN, preferred_element_type=jnp.float32)[:32]
     odd = lax.dot_general(odd_hot, own_hot, TN, preferred_element_type=jnp.float32)[:32]
-    pick_v[...] = jnp.concatenate([even] * 3 + [odd] * 3, axis=0).astype(jnp.bfloat16)
+    pick_v[...] = jnp.concatenate([even] * 3 + [odd] * 3, axis=0).T.astype(jnp.bfloat16)
     acc[...] = jnp.zeros_like(acc)
 
     def answer(g):
@@ -323,6 +323,7 @@
 
     lanes = lax.broadcasted_iota(jnp.int32, (DEVICES, 128), 1)
     into = jnp.where(name_in[:, 0, :] == (lanes + 1).astype(jnp.float32), 1.0, 0.0)
+    turned = jnp.concatenate([into.T[:OWN]] * 3, axis=1).astype(jnp.bfloat16)
     into = into.astype(jnp.bfloat16)
     ones = jnp.ones((DEVICES, 128), jnp.bfloat16)
     tally = lax.dot_general(into, ones, TN, preferred_element_type=jnp.float32)
@@ -360,17 +361,16 @@
 
     sums = jnp.sum(acc[...], axis=1)
     parts = jnp.concatenate(split3(sums[:, :128]) + split3(sums[:, 128:]), axis=0)
-    part_out[:, 0, :] = lax.dot_general(pick_v[...], parts, TN, preferred_element_type=jnp.float32)
+    part_out[:, 0, :] = jnp.dot(pick_v[...], parts, preferred_element_type=jnp.float32)
     for i in range(SELF):
         send(part_out, part_in, i, i, part_sems.at[0], part_sems.at[1])
     keep(part_out, part_in, part_sems.at[1])
-    into = jnp.concatenate([into] * 3, axis=0)
     got(name_out, name_in, 0, SELF, name_sems.at[3])
     got(row_out, row_in, 0, SELF, row_sems.at[0])
     got(part_out, part_in, 0, DEVICES, part_sems.at[1])
     arrived = jnp.concatenate(split3(part_in[:, 0, :]), axis=0)
-    total = lax.dot_general(into, arrived, TN, preferred_element_type=jnp.float32)
-    total_ref[...] = total[:OWN]
+    total = jnp.dot(turned, arrived, preferred_element_type=jnp.float32)
+    total_ref[...] = total
     got(part_out, part_in, 0, SELF, part_sems.at[0])
 
 
@@ -408,7 +408,7 @@
             pltpu.VMEM((8, 128), jnp.int32),
             pltpu.SMEM((8, 128), jnp.int32),
             pltpu.VMEM((32, 8, 256), f32),
-            pltpu.VMEM((6 * 32, 128), jnp.bfloat16),
+            pltpu.VMEM((128, 6 * 32), jnp.bfloat16),
         ]
         + [pltpu.VMEM((256, WINDOW), jnp.bfloat16)] * NBANDS
         + [dma((12,)), dma, dma((2,)), dma((2,)), dma((4,)), dma((2,)), dma((2,))],

time: 36.8 us -> 36.6 us (level)
  no operation moved by 1% of the time
where the time goes in v6:
time: 36.6 us; the launch traced here: 36.5 us
  Pallas kernels  34.5 us (94%)
  other arithmetic  1.32 us (4%)
  between operations  0.66 us (2%)
    pallas_call x1, Pallas kernels, shards(): pl.pallas_call(kernel, out_shape=(out, out), in_specs=[hbm] * 7, out_spec...  34.5 us
    div x1, other arithmetic, shards(): return total / jnp.sqrt(jnp.maximum(tally, 1.0) * CHAN)  1.32 us

profile of v6, /device:TPU:1, one launch (start us, length us, event | category | flops | bytes accessed | tf_op | source)
XLA Modules:
  0.0 36.5 jit_solution(7398614991104216737)
XLA Ops:
  0.7 34.5 %match.1 = (f32[16,128]{1,0:T(8,128)}, f32[16,128]{1,0:T(8,128)}) custom-call(f32[899,768]{1,0:T(8,128)} %bitcast.2, f32[3,5]{1,0:T(4,128)} %stencil_hbm.1, f32[768]{0:T(1024)} %mad_hbm.1, bf16[16,512]{1,0:T(8,128)(2,1)} %templates_hbm.1, s32[2048]{0:T(1024)} %bitcast.3, s32[1,32]{1,0:T(1,128)} %listed_hbm.1, s32[1,1]{1,0:T(1,128)S(6)} %copy.8.counts_hbm), custom_call_target="tpu_custom_call" | custom-call | tf_op jit(solution)/shard_map/match/pallas_call | solution.py:383
  35.1 1.3 %rsqrt_multiply_fusion = f32[16,128]{1,0:T(8,128)} fusion(f32[16,128]{1,0:T(8,128)} %get-tuple-element.7, f32[16,128]{1,0:T(8,128)} %get-tuple-element.8), kind=kLoop, calls=%fused_computation | loop fusion | flops 6144 | bytes 24576 | tf_op jit(solution)/shard_map/div | solution.py:420
